TPU v7x, 256 devices: a whole 4x4x8 slice. The times are simulated.
256 devices in a mesh: section: 16 (over z_hi, x), dp: 4 (over y), tensor: 4 (over z_lo, core).
Axes of the slice: x: 4, y: 4, z: 8 (z_hi: 4, z_lo: 2; z = z_hi * 2 + z_lo), core: 2. Of those that a mesh axis runs over, the one named last changes fastest.
Arguments:
- context: bfloat16 [16, 1024, 3072], P('section', 'dp', 'tensor'), may hold values from -6 to 6
- out_weight: bfloat16 [16, 6144, 3072], P('section', 'dp', 'tensor'), may hold values from -0.109375 to 0.109375
- residual: bfloat16 [16, 1024, 6144], P('section', 'dp', 'tensor'), may hold values from -6 to 6
- send_table: bfloat16 [16, 16, 128, 6144], P('section', 'dp', None, 'tensor'), may hold values from -6 to 6
- recv_table: bfloat16 [16, 16, 128, 6144], P('section', 'dp', None, 'tensor'), may hold values from -52 to 52
- sample_ids: int32 [8], P('dp'), may hold values from 0 to 3, as said below
- norm_gain: float32 [16, 6144], P('section', 'tensor'), may hold values from 0.5 to 1.5
- norm_bias: float32 [16, 6144], P('section', 'tensor'), may hold values from -3 to 3
- cotangent: bfloat16 [16, 1024, 6144], P('section', 'dp', 'tensor'), may hold values from -5.2 to 5.2
Outputs:
- refreshed: bfloat16 [16, 1024, 6144], P('section', 'dp', 'tensor')
- normed: bfloat16 [16, 1024, 6144], P('section', 'dp', 'tensor')
- weight_grad: bfloat16 [16, 6144, 3072], P('section', 'dp', 'tensor')
- context_grad: bfloat16 [16, 1024, 3072], P('section', 'dp', 'tensor')
Inputs may be any that keep to these rules, and one draw needn't show every extreme that they name: `sample_ids`: within the 2 entries of one replica the ids are distinct.
All inputs are finite; a program needn't handle non-finite values. Where the computation divides by a largest or mean magnitude, that divisor is 1e-20 or more.
Results may differ from a plain program's by a relative error of at most 0.015.
Values may be sent and summed in bfloat16 or wider, within the bound.
No kernel may reach another device: no remote copies, remote signals or barrier semaphores. Data moves between devices by JAX's collectives and lax.ppermute only.
A program may use at most 128 MiB of HBM per device.

v0:
```python
import jax
import jax.numpy as jnp
from jax import lax
from jax.sharding import PartitionSpec as P

BLK = 128


def shifted(x, axis, by):
    devices = lax.axis_size(axis)
    return lax.ppermute(x, axis, [(i, (i + by) % devices) for i in range(devices)])


def quantize(values):
    count_rows, count_cols = values.shape
    blocks = values.reshape(count_rows, count_cols // BLK, BLK)
    scales = (jnp.max(jnp.abs(blocks), axis=2) + 1e-06).astype(jnp.bfloat16)
    coded = (blocks / scales.astype(jnp.float32)[:, :, None]).astype(jnp.bfloat16)
    return (coded.reshape(count_rows, count_cols), scales)


def dequantize(coded, scales):
    count_rows, count_cols = coded.shape
    blocks = coded.astype(jnp.float32).reshape(count_rows, count_cols // BLK, BLK)
    return (blocks * scales.astype(jnp.float32)[:, :, None]).reshape(count_rows, count_cols)


def body(
    context,
    out_weight,
    residual,
    send_table,
    recv_table,
    sample_ids,
    norm_gain,
    norm_bias,
    cotangent,
):
    ctx_local = context[0]
    weight = out_weight[0]
    tok_rows = ctx_local.shape[0]
    local_cols = residual.shape[2]
    full_width = local_cols * lax.axis_size("tensor")
    contract_last = (((1,), (1,)), ((), ()))
    whole_weight = lax.all_gather(weight, "dp", axis=0, tiled=True)
    head_terms = lax.dot_general(
        ctx_local, whole_weight, contract_last, preferred_element_type=jnp.float32
    ).astype(jnp.bfloat16)
    summed = lax.psum_scatter(head_terms, "tensor", scatter_dimension=1, tiled=True).astype(
        jnp.float32
    )
    boundary = residual[0].astype(jnp.float32) + summed
    stored = send_table[0][sample_ids].reshape(tok_rows, local_cols)
    quantized, scales = quantize(boundary - stored.astype(jnp.float32))
    arrived_codes, arrived_scales = shifted((quantized, scales), "section", 1)
    received = recv_table[0][sample_ids].reshape(tok_rows, local_cols)
    refreshed = (received.astype(jnp.float32) + dequantize(arrived_codes, arrived_scales)).astype(
        jnp.bfloat16
    )
    row_vals = refreshed.astype(jnp.float32)
    row_sums = lax.psum((jnp.sum(row_vals, axis=1), jnp.sum(row_vals * row_vals, axis=1)), "tensor")
    row_mean = row_sums[0][:, None] / full_width
    variance = row_sums[1][:, None] / full_width - row_mean * row_mean
    inverse = lax.rsqrt(variance + 1e-05)
    normalized = (row_vals - row_mean) * inverse
    normed = (normalized * norm_gain[0] + norm_bias[0]).astype(jnp.bfloat16)
    scaled_grad = cotangent[0].astype(jnp.float32) * norm_gain[0]
    grad_sums = lax.psum(
        (jnp.sum(scaled_grad, axis=1), jnp.sum(scaled_grad * normalized, axis=1)), "tensor"
    )
    grad_in = inverse * (
        scaled_grad
        - grad_sums[0][:, None] / full_width
        - normalized * (grad_sums[1][:, None] / full_width)
    )
    grad_codes, grad_scales = quantize(grad_in)
    gathered_grad = (
        lax.all_gather(grad_codes, "tensor", axis=1, tiled=True),
        lax.all_gather(grad_scales, "tensor", axis=1, tiled=True),
    )
    returned = shifted((gathered_grad[0], gathered_grad[1]), "section", -1)
    grad_whole = dequantize(returned[0], returned[1]).astype(jnp.bfloat16)
    ctx_grad = jnp.dot(grad_whole, whole_weight, preferred_element_type=jnp.float32)
    weight_grad = lax.psum_scatter(
        lax.dot_general(
            grad_whole, ctx_local, (((0,), (0,)), ((), ())), preferred_element_type=jnp.float32
        ).astype(jnp.bfloat16),
        "dp",
        scatter_dimension=0,
        tiled=True,
    )
    return (refreshed[None], normed[None], weight_grad[None], ctx_grad.astype(jnp.bfloat16)[None])


def solution(mesh):
    return jax.shard_map(
        body,
        mesh=mesh,
        in_specs=(
            P("section", "dp", "tensor"),
            P("section", "dp", "tensor"),
            P("section", "dp", "tensor"),
            P("section", "dp", None, "tensor"),
            P("section", "dp", None, "tensor"),
            P("dp"),
            P("section", "tensor"),
            P("section", "tensor"),
            P("section", "dp", "tensor"),
        ),
        out_specs=(
            P("section", "dp", "tensor"),
            P("section", "dp", "tensor"),
            P("section", "dp", "tensor"),
            P("section", "dp", "tensor"),
        ),
        check_vma=False,
    )
```

profile of v0, /device:TPU:17, one launch (start us, length us, event | category | flops | bytes accessed | tf_op | source)
XLA Modules:
  0.0 533.1 jit_solution(13004598329995477894)
XLA Ops:
  7.2 0.0 all-gather.7.cloned.1.call-start
  7.2 0.7 all-gather.7.cloned.1.call-update
  7.9 0.0 reduce-scatter.3.cloned.1.call-start
  8.0 98.9 %all-gather.7.cloned.1.call-done = bf16[1,6144,768]{2,1,0:T(8,128)(2,1)} async-done(((bf16[1,1536,768]{2,1,0:T(8,128)(2,1)}), bf16[1,6144,768]{2,1,0:T(8,128)(2,1)}) %all-gather.7.cloned.1.call-update) | async-done | bytes 9437200 | tf_op jit(solution)/shard_map/all_gather | solution.py:45
  106.9 11.1 %fusion.4 = bf16[256,6144]{1,0:T(8,128)(2,1)} fusion(bf16[1,6144,768]{2,1,0:T(8,128)(2,1)} %all-gather.7.cloned.1.call-done, bf16[1,256,768]{2,1,0:T(8,128)(2,1)S(1)} %copy-done.6), kind=kOutput, calls=%fused_computation.7 | convolution fusion | flops 2417491968 | bytes 12976128 | tf_op jit(solution)/shard_map/dot_general | solution.py:46
  118.1 0.0 all-gather.5.cloned.1.call-start
  118.1 0.6 copy-done.17
  118.7 0.6 gather_fusion.1
  119.3 39.9 %reduce-scatter.3.cloned.1.call-done = bf16[256,1536]{1,0:T(8,128)(2,1)} async-done(((bf16[256,6144]{1,0:T(8,128)(2,1)}), bf16[256,1536]{1,0:T(8,128)(2,1)}) %reduce-scatter.3.cloned.1.call-update) | async-done | bytes 786448 | tf_op jit(solution)/shard_map/reduce_scatter | solution.py:49
  159.2 2.6 fusion.27
  161.8 1.9 copy.20
  163.7 0.1 reduce_max.18
  163.8 0.6 copy-done.8
  164.4 0.1 div.34
  164.5 1.6 copy.21
  166.1 3.0 divide_convert_fusion.1
  169.2 1.2 collective-permute-start
  170.3 1.2 collective-permute-start.1
  171.5 0.7 reduce
  172.3 1.3 reduce.1
  173.6 1.6 gather_fusion
  175.2 21.8 %collective-permute-done.1 = bf16[256,12]{0,1:T(8,128)(2,1)S(1)} collective-permute-done((bf16[256,12]{0,1:T(8,128)(2,1)S(1)}, bf16[256,12]{0,1:T(8,128)(2,1)S(1)}, u32[]{:S(2)}, u32[]{:S(2)}) %collective-permute-start.1) | collective-permute-done | bytes 6176 | tf_op jit(solution)/shard_map/ppermute | solution.py:11
  197.0 0.1 mul.70
  197.1 0.5 copy.22
  197.6 1.9 convert_reduce_fusion
  199.5 17.9 %all-reduce.1 = (f32[256]{0:T(256)S(1)}, f32[256]{0:T(256)S(1)}) all-reduce(f32[256]{0:T(256)S(1)} %get-tuple-element.7, f32[256]{0:T(256)S(1)} %get-tuple-element.6), channel_id=1, replica_groups=mesh['section'=16,'dp'=4,'tensor'=4] {'tensor'}, use_global_device_ids=true, to_apply=%region_5.0 | all-reduce | flops 512 | bytes 4096 | tf_op jit(solution)/shard_map/psum | solution.py:61
  217.5 0.5 fusion.19
  218.0 6.6 %all-reduce = (f32[256]{0:T(256)S(1)}, f32[256]{0:T(256)S(1)}) all-reduce(f32[256]{0:T(256)S(1)} %get-tuple-element.5, f32[256]{0:T(256)S(1)} %get-tuple-element.4), channel_id=1, replica_groups=mesh['section'=16,'dp'=4,'tensor'=4] {'tensor'}, use_global_device_ids=true, to_apply=%region_9.0 | all-reduce | flops 512 | bytes 4096 | tf_op jit(solution)/shard_map/psum | solution.py:68
  224.6 0.6 copy-done.14
  225.2 1.7 fusion.28
  226.9 1.9 copy.23
  228.8 0.7 reduce_max.19
  229.5 1.3 fusion.33
  230.8 0.1 div.41
  230.9 1.6 copy.24
  232.5 3.4 divide_convert_fusion
  236.0 0.0 reduce-scatter.5.cloned.1.call-start
  236.0 39.7 %all-gather.5.cloned.1.call-done = bf16[256,6144]{1,0:T(8,128)(2,1)} async-done(((bf16[256,1536]{1,0:T(8,128)(2,1)}), bf16[256,6144]{1,0:T(8,128)(2,1)}) %all-gather.5.cloned.1.call-update) | async-done | bytes 3145744 | tf_op jit(solution)/shard_map/all_gather | solution.py:78
  275.8 5.1 collective-permute-start.2
  280.8 139.9 %all-gather.1 = bf16[4,12,256]{2,1,0:T(8,128)(2,1)S(1)} all-gather(bf16[1,12,256]{2,1,0:T(8,128)(2,1)S(1)} %copy-done.11), channel_id=1, replica_groups=mesh['section'=16,'dp'=4,'tensor'=4] {'tensor'}, dimensions={0}, use_global_device_ids=true | all-gather | bytes 30720 | tf_op jit(solution)/shard_map/all_gather | solution.py:79
  420.7 0.3 collective-permute-start.3
  421.0 2.7 collective-permute-done.3
  423.6 0.1 copy.25
  423.8 1.8 mul.85
  425.6 2.6 copy-done.2
  428.1 10.0 %convolution_convert_fusion = bf16[6144,768]{1,0:T(8,128)(2,1)} fusion(bf16[1,256,768]{2,1,0:T(8,128)(2,1)S(1)} %copy-done.6, f32[32,8,48,128]{3,2,1,0:T(8,128)S(1)} %bitcast.60, bf16[256,6144]{1,0:T(8,128)(2,1)} %collective-permute-done.2), kind=kOutput, calls=%fused_computation.2 | convolution fusion | flops 2425356288 | bytes 19267584 | tf_op jit(solution)/shard_map/dot_general | solution.py:85
  438.2 11.2 %fusion.24 = bf16[1,256,768]{2,1,0:T(8,128)(2,1)} fusion(bf16[1,6144,768]{2,1,0:T(8,128)(2,1)} %all-gather.7.cloned.1.call-done, f32[32,8,48,128]{3,2,1,0:T(8,128)} %bitcast.61, bf16[256,6144]{1,0:T(8,128)(2,1)} %collective-permute-done.2), kind=kOutput, calls=%fused_computation.33 | convolution fusion | flops 2420834304 | bytes 19267584 | tf_op jit(solution)/shard_map/dot_general | solution.py:83
  449.4 77.2 %reduce-scatter.5.cloned.1.call-done = bf16[1536,768]{1,0:T(8,128)(2,1)} async-done(((bf16[6144,768]{1,0:T(8,128)(2,1)}), bf16[1536,768]{1,0:T(8,128)(2,1)}) %reduce-scatter.5.cloned.1.call-update) | async-done | bytes 2359312 | tf_op jit(solution)/shard_map/reduce_scatter | solution.py:84
  (43 shorter events, 0.2 us)
Async XLA Ops:
  7.2 111.5 %copy-start = (bf16[1,4,128,1536]{3,2,1,0:T(8,128)(2,1)S(1)}, bf16[1,4,128,1536]{3,2,1,0:T(8,128)(2,1)}, u32[]{:S(2)}) copy-start(bf16[1,4,128,1536]{3,2,1,0:T(8,128)(2,1)} %param.12) | copy-start | bytes 4718596
  7.2 99.7 %copy-start.6 = (bf16[1,256,768]{2,1,0:T(8,128)(2,1)S(1)}, bf16[1,256,768]{2,1,0:T(8,128)(2,1)}, u32[]{:S(2)}) copy-start(bf16[1,256,768]{2,1,0:T(8,128)(2,1)} %param.9) | copy-start | bytes 1179652
  7.2 99.7 %all-gather.7.cloned.1.call-start = ((), (), s32[]{:S(2)}) async-start(), calls=%async_computation.5 | async-start | bytes 11796480 | tf_op jit(solution)/shard_map/all_gather | solution.py:45
  7.9 151.3 %reduce-scatter.3.cloned.1.call-start = ((), (), s32[]{:S(2)}) async-start(), calls=%async_computation.2 | async-start | bytes 3932160 | tf_op jit(solution)/shard_map/reduce_scatter | solution.py:49
  118.0 0.7 copy-start.17
  118.1 41.1 %copy-start.5 = (bf16[1,256,1536]{2,1,0:T(8,128)(2,1)S(1)}, bf16[1,256,1536]{2,1,0:T(8,128)(2,1)}, u32[]{:S(2)}) copy-start(bf16[1,256,1536]{2,1,0:T(8,128)(2,1)} %param.11) | copy-start | bytes 2359300
  118.1 157.7 %all-gather.5.cloned.1.call-start = ((), (), s32[]{:S(2)}) async-start(), calls=%async_computation.3 | async-start | bytes 3932160 | tf_op jit(solution)/shard_map/all_gather | solution.py:78
  118.7 43.1 %copy-start.16 = (s32[1024]{0:T(1024)}, s32[1024]{0:T(1024)S(1)}, u32[]{:S(2)}) copy-start(s32[1024]{0:T(1024)S(1)} %pad_clamp_fusion) | copy-start | bytes 12292
  163.8 0.6 copy-start.8
  166.1 4.2 copy-start.9
  166.1 7.4 %copy-start.7 = (bf16[1,4,128,1536]{3,2,1,0:T(8,128)(2,1)S(1)}, bf16[1,4,128,1536]{3,2,1,0:T(8,128)(2,1)}, u32[]{:S(2)}) copy-start(bf16[1,4,128,1536]{3,2,1,0:T(8,128)(2,1)} %param.13) | copy-start | bytes 4718596
  169.2 28.4 %collective-permute-start = (bf16[256,1536]{1,0:T(8,128)(2,1)}, bf16[256,1536]{1,0:T(8,128)(2,1)}, u32[]{:S(2)}, u32[]{:S(2)}) collective-permute-start(bf16[256,1536]{1,0:T(8,128)(2,1)} %divide_convert_fusion.1), channel_id=1, source_target_pairs={{0,16},{16,32},{32,48},{48,64},{64,80},{80,96},{96,112},{112,128},... | collective-permute-start | bytes 2359304 | tf_op jit(solution)/shard_map/ppermute | solution.py:11
  170.3 26.6 %collective-permute-start.1 = (bf16[256,12]{0,1:T(8,128)(2,1)S(1)}, bf16[256,12]{0,1:T(8,128)(2,1)S(1)}, u32[]{:S(2)}, u32[]{:S(2)}) collective-permute-start(bf16[256,12]{0,1:T(8,128)(2,1)S(1)} %copy-done.9), channel_id=1, source_target_pairs={{0,16},{16,32},{32,48},{48,64},{64,80},{80,96},{96,112},{112,128},... | collective-permute-start | bytes 18440 | tf_op jit(solution)/shard_map/ppermute | solution.py:11
  197.6 19.9 %copy-start.4 = (bf16[1,256,1536]{2,1,0:T(8,128)(2,1)S(1)}, bf16[1,256,1536]{2,1,0:T(8,128)(2,1)}, u32[]{:S(2)}) copy-start(bf16[1,256,1536]{2,1,0:T(8,128)(2,1)} %param.17) | copy-start | bytes 2359300
  199.5 33.0 %copy-start.3 = (bf16[256,1536]{1,0:T(8,128)(2,1)}, bf16[256,1536]{1,0:T(8,128)(2,1)S(1)}, u32[]{:S(2)}) copy-start(bf16[256,1536]{1,0:T(8,128)(2,1)S(1)} %get-tuple-element.12) | copy-start | bytes 2359300
  217.5 7.1 %copy-start.12 = (f32[256]{0:T(256)}, f32[256]{0:T(256)S(1)}, u32[]{:S(2)}) copy-start(f32[256]{0:T(256)S(1)} %get-tuple-element.17) | copy-start | bytes 3076
  217.5 7.1 %copy-start.13 = (f32[256]{0:T(256)}, f32[256]{0:T(256)S(1)}, u32[]{:S(2)}) copy-start(f32[256]{0:T(256)S(1)} %get-tuple-element.18) | copy-start | bytes 3076
  224.6 0.6 copy-start.14
  224.6 0.6 copy-start.15
  230.9 1.6 copy-start.10
  232.5 48.3 %copy-start.11 = (bf16[1,12,256]{2,1,0:T(8,128)(2,1)S(1)}, bf16[1,12,256]{2,1,0:T(8,128)(2,1)}, u32[]{:S(2)}) copy-start(bf16[1,12,256]{2,1,0:T(8,128)(2,1)} %get-tuple-element.16) | copy-start | bytes 18436
  236.0 290.6 %reduce-scatter.5.cloned.1.call-start = ((), (), s32[]{:S(2)}) async-start(), calls=%async_computation.4 | async-start | bytes 11796480 | tf_op jit(solution)/shard_map/reduce_scatter | solution.py:84
  275.8 148.0 %collective-permute-start.2 = (bf16[256,6144]{1,0:T(8,128)(2,1)}, bf16[256,6144]{1,0:T(8,128)(2,1)}, u32[]{:S(2)}, u32[]{:S(2)}) collective-permute-start(bf16[256,6144]{1,0:T(8,128)(2,1)} %all-gather.5.cloned.1.call-done), channel_id=1, source_target_pairs={{0,240},{16,0},{32,16},{48,32},{64,48},{80,64},{96,80},{112,96},{1... | collective-permute-start | bytes 9437192 | tf_op jit(solution)/shard_map/ppermute | solution.py:11
  420.7 2.9 collective-permute-start.3
  425.5 2.6 copy-start.2
  438.1 88.4 %copy-start.1 = (bf16[1,4,128,1536]{3,2,1,0:T(8,128)(2,1)S(1)}, bf16[1,4,128,1536]{3,2,1,0:T(8,128)(2,1)}, u32[]{:S(2)}) copy-start(bf16[1,4,128,1536]{3,2,1,0:T(8,128)(2,1)} %param.12) | copy-start | bytes 4718596
Sparse Core Ops, SparseCore 0:
  9.8 97.0 all-gather.6
  118.2 40.9 reduce-scatter.2
  236.1 39.6 all-gather.4
  438.3 88.2 reduce-scatter.4
where the time goes:
time: 536 us; the launch traced here: 533 us
  waiting for transfers between devices  281 us (52%)
  blocking collectives  164 us (31%)
  matrix products  32.3 us (6%)
  other arithmetic  17.4 us (3%)
  local copies, waits for them, and re-layouts  16.3 us (3%)
  between operations  14 us (3%)
  starting transfers between devices  7.87 us (1%)
    all_gather x1, blocking collectives, body(): lax.all_gather(grad_scales, 'tensor', axis=1, tiled=True)  140 us
    all_gather x1, waiting for transfers between devices, body(): whole_weight = lax.all_gather(weight, 'dp', axis=0, tiled=True)  98.9 us
    reduce_scatter x1, waiting for transfers between devices, body(): lax.psum_scatter(lax.dot_general(grad_whole, ctx_local, (((0,), (0,)), ((...  77.2 us
    reduce_scatter x1, waiting for transfers between devices, body(): lax.psum_scatter(head_terms, 'tensor', scatter_dimension=1, tiled=True)  39.9 us
    all_gather x1, waiting for transfers between devices, body(): lax.all_gather(grad_codes, 'tensor', axis=1, tiled=True)  39.7 us
    ppermute x4, waiting for transfers between devices, shifted(): lax.ppermute(x, axis, [(i, (i + by) % devices) for i in range(devices)])  24.5 us
    psum x1, blocking collectives, body(): lax.psum((jnp.sum(row_vals, axis=1), jnp.sum(row_vals * row_vals, axis=1)...  17.9 us
    dot_general x1, matrix products, body(): jnp.dot(grad_whole, whole_weight, preferred_element_type=jnp.float32)  11.2 us
  transfers between devices with their start and end apart: 8, of which 6 were waited for; matrix products, arithmetic and copies ran while one was open for 3% of the time, Pallas kernels for 0%

commit v1 on v0

v1 whole, which is shorter than its diff:
```python
import functools
import jax
import jax.numpy as jnp
from jax import lax
from jax.experimental import pallas as pl
from jax.experimental.pallas import tpu as pltpu
from jax.sharding import PartitionSpec as P

BLK = 128
ROWS = 128
GROUP = 16
RING = 4
ALL = ("section", "dp", "tensor")
F32 = jnp.float32
BF16 = jnp.bfloat16
LAST = (((1,), (1,)), ((), ()))
FIRST = (((0,), (0,)), ((), ()))
PLAIN = (((1,), (0,)), ((), ()))


def params(mib=32):
    return pltpu.CompilerParams(vmem_limit_bytes=mib * 1024 * 1024)


def cost(flops, nbytes):
    return pl.CostEstimate(flops=flops, bytes_accessed=nbytes, transcendentals=0)


def crossed(x, k, axis="tensor"):
    n = lax.axis_size(axis)
    return lax.ppermute(x, axis, [(i, i ^ k) for i in range(n)])


def after(x, done):
    return x if done is None else lax.optimization_barrier((x, done))[0]


def added(*terms):
    return sum(v.astype(F32) for v in terms).astype(BF16)


def coded(values):
    largest = jnp.max(jnp.abs(values), axis=1, keepdims=True)
    scale = (jnp.broadcast_to(largest, values.shape) + 1e-06).astype(BF16).astype(F32)
    code = (values / scale).astype(BF16).astype(F32)
    return code * scale


def whole(shape):
    return pl.BlockSpec(shape, lambda *_: (0,) * len(shape))


def head_kernel(a00, a01, a10, a11, mine_ref, other_ref, p0, p1):
    prod = lax.dot_general(
        jnp.concatenate([a00[...], a10[...]], axis=0), mine_ref[...], LAST, preferred_element_type=F32
    ) + lax.dot_general(
        jnp.concatenate([a01[...], a11[...]], axis=0), other_ref[...], LAST, preferred_element_type=F32
    )
    rows = p0.shape[0]
    p0[...] = prod[:rows].astype(BF16)
    p1[...] = prod[rows:].astype(BF16)


def head(blocks, weight, other):
    feats, width = weight.shape
    rows = blocks[0].shape[0]
    tile = 256
    return pl.pallas_call(
        head_kernel,
        grid=(feats // tile,),
        in_specs=[whole((rows, width))] * 4 + [pl.BlockSpec((tile, width), lambda j: (j, 0))] * 2,
        out_specs=[pl.BlockSpec((rows, tile), lambda j: (0, j))] * 2,
        out_shape=[jax.ShapeDtypeStruct((rows, feats), BF16)] * 2,
        compiler_params=params(),
        cost_estimate=cost(8 * rows * width * feats, 4 * (feats * width + rows * (2 * width + feats))),
        name="head",
    )(*blocks, weight, other)


def pick_kernel(ids, table_ref, out_ref):
    out_ref[...] = table_ref[0]


def pick(ids, table):
    cols = table.shape[2]
    return pl.pallas_call(
        pick_kernel,
        grid_spec=pltpu.PrefetchScalarGridSpec(
            num_scalar_prefetch=1,
            grid=(ids.shape[0],),
            in_specs=[pl.BlockSpec((1, ROWS, cols), lambda b, ids: (ids[b], 0, 0))],
            out_specs=pl.BlockSpec((ROWS, cols), lambda b, ids: (b, 0)),
        ),
        out_shape=jax.ShapeDtypeStruct((ids.shape[0] * ROWS, cols), BF16),
        compiler_params=params(),
        cost_estimate=cost(1, ids.shape[0] * ROWS * cols * 4),
        name="pick",
    )(ids, table)


def sums_kernel(ids, y0, y1, res_ref, table_ref, recv_ref, cot_ref, gain_ref, out_ref, delta_ref, stat_ref, held):
    rows, cols = out_ref.shape
    for r in range(0, rows, GROUP):
        total = [jnp.zeros((GROUP, BLK), F32)] * 4
        for c in range(0, cols, BLK):
            at = (slice(r, r + GROUP), slice(c, c + BLK))
            boundary = res_ref[at].astype(F32) + (y0[at].astype(F32) + y1[at].astype(F32))
            delta = coded(boundary - table_ref[0, at[0], at[1]].astype(F32)).astype(BF16)
            delta_ref[at] = delta
            fresh = (recv_ref[at].astype(F32) + delta.astype(F32)).astype(BF16)
            out_ref[at] = fresh
            x = fresh.astype(F32)
            g = cot_ref[at].astype(F32) * gain_ref[:, at[1]]
            for i, v in enumerate((x, x * x, g, g * x)):
                total[i] = total[i] + v
        for i in range(4):
            held[i, r : r + GROUP, :] = total[i]
    for i in range(4):
        stat_ref[i : i + 1, :] = jnp.sum(held[i].T, axis=0, keepdims=True)
    stat_ref[4:8, :] = jnp.zeros((4, rows), F32)


def sums(ids, y0, y1, residual, table, recv, cot, gain):
    rows, cols = cot.shape
    chunk = pl.BlockSpec((ROWS, cols), lambda b, ids: (b, 0))
    return pl.pallas_call(
        sums_kernel,
        grid_spec=pltpu.PrefetchScalarGridSpec(
            num_scalar_prefetch=1,
            grid=(rows // ROWS,),
            in_specs=[chunk, chunk, chunk]
            + [pl.BlockSpec((1, ROWS, cols), lambda b, ids: (ids[b], 0, 0))]
            + [chunk, chunk, whole((1, cols))],
            out_specs=[chunk, chunk, pl.BlockSpec((8, ROWS), lambda b, ids: (b, 0))],
            scratch_shapes=[pltpu.VMEM((4, ROWS, BLK), F32)],
        ),
        out_shape=[
            jax.ShapeDtypeStruct((rows, cols), BF16),
            jax.ShapeDtypeStruct((rows, cols), BF16),
            jax.ShapeDtypeStruct((rows // ROWS * 8, ROWS), F32),
        ],
        compiler_params=params(),
        cost_estimate=cost(rows * cols * 20, rows * cols * 14),
        name="sums",
    )(ids, y0, y1, residual, table, recv, cot, gain)


def moments(stat, held):
    rows = held.shape[1]
    mean = stat[0:1]
    inverse = lax.rsqrt(stat[1:2] - mean * mean + 1e-05)
    grad_mean = stat[2:3]
    proj = (stat[3:4] - mean * grad_mean) * inverse
    for i, v in enumerate((mean, inverse, grad_mean, proj)[: held.shape[0]]):
        held[i] = jnp.broadcast_to(v, (rows, rows)).T


def norm_kernel(full, s0, s1, s2, s3, x_ref, cot_ref, gain_ref, stat_ref, out_ref, held):
    rows, cols = x_ref.shape
    stat_ref[...] = (s0[...] + s1[...] + s2[...] + s3[...]) / full
    moments(stat_ref[...], held)
    for r in range(0, rows, GROUP):
        mean, inverse, grad_mean, proj = (held[i, r : r + GROUP, :] for i in range(4))
        for c in range(0, cols, BLK):
            at = (slice(r, r + GROUP), slice(c, c + BLK))
            normalized = (x_ref[at].astype(F32) - mean) * inverse
            grad = cot_ref[at].astype(F32) * gain_ref[:, at[1]] - grad_mean - normalized * proj
            out_ref[at] = coded(inverse * grad).astype(BF16)


def norm(full, stats, x, cot, gain):
    rows, cols = x.shape
    chunk = pl.BlockSpec((ROWS, cols), lambda b: (b, 0))
    stat = pl.BlockSpec((8, ROWS), lambda b: (b, 0))
    return pl.pallas_call(
        functools.partial(norm_kernel, full),
        grid=(rows // ROWS,),
        in_specs=[stat] * 4 + [chunk, chunk, whole((1, cols))],
        out_specs=[stat, chunk],
        out_shape=[
            jax.ShapeDtypeStruct(stats[0].shape, F32),
            jax.ShapeDtypeStruct((rows, cols), BF16),
        ],
        scratch_shapes=[pltpu.VMEM((4, ROWS, ROWS), F32)],
        compiler_params=params(),
        cost_estimate=cost(rows * cols * 20, rows * cols * 6),
        name="norm",
    )(*stats, x, cot, gain)


def finish_kernel(ids, delta_ref, table_ref, stat_ref, gain_ref, bias_ref, fresh_ref, norm_ref, held):
    moments(stat_ref[...], held)
    rows, cols = fresh_ref.shape
    for r in range(0, rows, GROUP):
        mean, inverse = (held[i, r : r + GROUP, :] for i in range(2))
        for c in range(0, cols, BLK):
            at = (slice(r, r + GROUP), slice(c, c + BLK))
            received = table_ref[0, at[0], at[1]].astype(F32)
            fresh = (received + delta_ref[at].astype(F32)).astype(BF16)
            fresh_ref[at] = fresh
            normalized = (fresh.astype(F32) - mean) * inverse
            norm_ref[at] = (normalized * gain_ref[:, at[1]] + bias_ref[:, at[1]]).astype(BF16)


def finish(ids, delta, table, stat, gain, bias):
    rows, cols = delta.shape
    chunk = pl.BlockSpec((ROWS, cols), lambda b, ids: (b, 0))
    return pl.pallas_call(
        finish_kernel,
        grid_spec=pltpu.PrefetchScalarGridSpec(
            num_scalar_prefetch=1,
            grid=(rows // ROWS,),
            in_specs=[
                chunk,
                pl.BlockSpec((1, ROWS, cols), lambda b, ids: (ids[b], 0, 0)),
                pl.BlockSpec((8, ROWS), lambda b, ids: (b, 0)),
                whole((1, cols)),
                whole((1, cols)),
            ],
            out_specs=[chunk, chunk],
            scratch_shapes=[pltpu.VMEM((2, ROWS, ROWS), F32)],
        ),
        out_shape=[jax.ShapeDtypeStruct((rows, cols), BF16)] * 2,
        compiler_params=params(),
        cost_estimate=cost(rows * cols * 8, rows * cols * 8),
        name="finish",
    )(ids, delta, table, stat, gain, bias)


def back_kernel(place, g0, g1, g2, g3, w_ref, e0, e1, e2, e3, held):
    grads = jnp.concatenate([g[...] for g in (g0, g1, g2, g3)], axis=0)
    prod = lax.dot_general(grads, w_ref[...], PLAIN, preferred_element_type=F32).astype(BF16)
    held[...] = prod.reshape(held.shape)
    for d, e in enumerate((e0, e1, e2, e3)):
        e[...] = held[jnp.bitwise_xor(place[0], d % 2) * 2 + jnp.bitwise_xor(place[1], d // 2)]


def back(place, grads, weight):
    feats, width = weight.shape
    rows = grads[0].shape[0]
    tile = 256
    return pl.pallas_call(
        back_kernel,
        grid_spec=pltpu.PrefetchScalarGridSpec(
            num_scalar_prefetch=1,
            grid=(width // tile,),
            in_specs=[whole((rows, feats))] * 4 + [pl.BlockSpec((feats, tile), lambda j, place: (0, j))],
            out_specs=[pl.BlockSpec((rows, tile), lambda j, place: (0, j))] * 4,
            scratch_shapes=[pltpu.VMEM((4, rows, tile), BF16)],
        ),
        out_shape=[jax.ShapeDtypeStruct((rows, width), BF16)] * 4,
        compiler_params=params(),
        cost_estimate=cost(8 * rows * width * feats, 2 * (feats * width + 4 * rows * (width + feats))),
        name="back",
    )(place, *grads, weight)


def weights_kernel(count, *refs):
    grads, ctx, out_ref = refs[:count], refs[count : 2 * count], refs[-1]
    lhs = jnp.concatenate([g[...] for g in grads], axis=0)
    rhs = jnp.concatenate([c[...] for c in ctx], axis=0)
    out_ref[...] = lax.dot_general(lhs, rhs, FIRST, preferred_element_type=F32).astype(BF16)


def weights(grads, blocks):
    count = len(grads)
    rows, feats = grads[0].shape
    width = blocks[0].shape[1]
    tile = 256
    return pl.pallas_call(
        functools.partial(weights_kernel, count),
        grid=(feats // tile,),
        in_specs=[pl.BlockSpec((rows, tile), lambda j: (0, j))] * count + [whole((rows, width))] * count,
        out_specs=pl.BlockSpec((tile, width), lambda j: (j, 0)),
        out_shape=jax.ShapeDtypeStruct((feats, width), BF16),
        compiler_params=params(),
        cost_estimate=cost(2 * count * rows * width * feats, 2 * (feats * width + count * rows * (width + feats))),
        name="weights",
    )(*grads, *blocks)


def body(
    context,
    out_weight,
    residual,
    send_table,
    recv_table,
    sample_ids,
    norm_gain,
    norm_bias,
    cotangent,
):
    n_sec, n_dp, n_ten = (lax.axis_size(a) for a in ALL)
    ctx, weight = context[0], out_weight[0]
    def index(z, x, q, r):
        return ((z % (n_sec // RING) * RING + x % RING) * n_dp + q) * n_ten + r

    places = [
        (z, x, q, r)
        for z in range(n_sec // RING)
        for x in range(RING)
        for q in range(n_dp)
        for r in range(n_ten)
    ]

    def sent(x, place, inverse=False):
        pairs = [(index(*p), index(*place(*p))) for p in places]
        return lax.ppermute(x, ALL, [(b, a) for a, b in pairs] if inverse else pairs)

    def owner(q, r, k):
        return q ^ (r % 2 + 2 * (k ^ (r // 2)))

    def spread(x, k, inverse=False):
        return sent(x, lambda z, x, q, r: (z, x, owner(q, r, k), q), inverse)

    def fetch(x, k, o):
        return sent(x, lambda z, x, q, r: (z, x, owner(q, r, k), r ^ o), True)

    def passed(x, step):
        wrap = RING - 1 if step > 0 else 0
        return sent(x, lambda z, x, q, r: (z + step * (x == wrap), x + step, q, r))

    def along(x, step):
        return sent(x, lambda z, x, q, r: (z, x + step, q, r))

    def across(x, step, first):
        column = (RING - 1 if step > 0 else 0) if first else (0 if step > 0 else RING - 1)
        return sent(x, lambda z, x, q, r: (z + step * (x == column), x, q, r))

    t = lax.axis_index("tensor")
    place = jnp.stack([t % 2, t // 2]).astype(jnp.int32)

    other = crossed(weight, 1)
    cot = along(cotangent[0], -1)
    columns = [fetch(ctx, 1, 0), fetch(ctx, 1, 1), fetch(ctx, 0, 1)]
    columns.append(fetch(after(ctx, (other, columns[0])), 0, 0))
    recv = across(after(pick(sample_ids, recv_table[0]), other), -1, True)
    prods = head([columns[i] for i in (3, 2, 0, 1)], weight, other)
    rest = [crossed(v, 1) for v in (columns[2], columns[1])]
    prods, rest = lax.optimization_barrier((prods, rest))
    y = [spread(u, k) for k, u in enumerate(prods)]
    cot = across(cot, -1, False)
    recv = along(recv, -1)
    gain = passed(after(norm_gain, prods), -1)

    x, delta, stat = sums(sample_ids, *y, residual[0], send_table[0], recv, cot, gain)
    delta = passed(delta, 1)
    stats = [stat] + [crossed(stat, k) for k in range(1, 4)]
    full = float(n_ten * residual.shape[2])
    stat, grad = norm(full, stats, x, cot, gain)
    stat = passed(stat, 1)
    grads = [spread(grad, k, True) for k in (0, 1)]
    grads = grads + [crossed(v, 1) for v in grads]
    mine, *terms = back(place, grads, weight)
    came = [crossed(e, d, "dp") for d, e in enumerate(terms, 1)]
    weight_grad = weights(grads, [columns[3], columns[0], *rest])
    refreshed, normed = finish(sample_ids, delta, recv_table[0], after(stat, weight_grad), norm_gain, norm_bias)
    came, weight_grad = lax.optimization_barrier((came, weight_grad))
    ctx_grad = added(mine, *came)

    return (refreshed[None], normed[None], weight_grad[None], ctx_grad[None])


def solution(mesh):
    rows = P("section", "dp", "tensor")
    table = P("section", "dp", None, "tensor")
    line = P("section", "tensor")
    return jax.shard_map(
        body,
        mesh=mesh,
        in_specs=(rows, rows, rows, table, table, P("dp"), line, line, rows),
        out_specs=(rows, rows, rows, rows),
        check_vma=False,
    )
```

time: 536 us -> 175 us (0.33)
  waiting for transfers between devices: 281 us -> 90.8 us
  blocking collectives: 164 us -> 0 us
  starting transfers between devices: 7.87 us -> 54.6 us
  matrix products: 32.3 us -> 0 us
  Pallas kernels: 0 us -> 23.3 us
  other arithmetic: 17.4 us -> 1.05 us
  between operations: 14 us -> 0.91 us
  local copies, waits for them, and re-layouts: 16.3 us -> 4.18 us
    all_gather x1 -> x0, blocking collectives: 140 us -> none  [body(): lax.all_gather(grad_scales, 'tensor', axis=1, tiled=True)]
    all_gather x2 -> x0, waiting for transfers between devices: 139 us -> none  [the longest x1 98.9 us: body(): whole_weight = lax.all_gather(weight, 'dp', axis=0, tiled=True)]
    reduce_scatter x2 -> x0, waiting for transfers between devices: 117 us -> none  [the longest x1 77.2 us: body(): lax.psum_scatter(lax.dot_general(grad_whole, ctx_local, (((0,), (0,)), ((...]
    ppermute x4 -> x26, waiting for transfers between devices: 24.5 us -> 90.8 us  [the longest x15 87.7 us: sent(): lax.ppermute(x, ALL, [(b, a) for a, b in pairs] if inverse else pairs)]
    ppermute x4 -> x26, starting transfers between devices: 7.71 us -> 54.6 us  [the longest x15 43.1 us: sent(): lax.ppermute(x, ALL, [(b, a) for a, b in pairs] if inverse else pairs)]
    dot_general x3 -> x0, matrix products: 32.3 us -> none  [the longest x1 11.2 us: body(): jnp.dot(grad_whole, whole_weight, preferred_element_type=jnp.float32)]
    psum x2 -> x0, blocking collectives: 24.5 us -> none  [the longest x1 17.9 us: body(): lax.psum((jnp.sum(row_vals, axis=1), jnp.sum(row_vals * row_vals, axis=1)...]
    pallas_call x0 -> x7, Pallas kernels: none -> 23.3 us  [the longest x1 7.02 us: weights(): pl.pallas_call(functools.partial(weights_kernel, count), grid=(feats // t...]
  transfers between devices with their start and end apart: 8 -> 26, of which waited for: 6 -> 11; matrix products, arithmetic and copies ran while one was open for 3% -> 0% of each run, Pallas kernels for 0% -> 11%
where the time goes in v1:
time: 175 us
  waiting for transfers between devices  90.8 us (52%)
  starting transfers between devices  54.6 us (31%)
  Pallas kernels  23.3 us (13%)
  local copies, waits for them, and re-layouts  4.18 us (2%)
    ppermute x15, waiting for transfers between devices, sent(): lax.ppermute(x, ALL, [(b, a) for a, b in pairs] if inverse else pairs)  87.7 us
    ppermute x15, starting transfers between devices, sent(): lax.ppermute(x, ALL, [(b, a) for a, b in pairs] if inverse else pairs)  43.1 us
    ppermute x11, starting transfers between devices, crossed(): return lax.ppermute(x, axis, [(i, i ^ k) for i in range(n)])  11.5 us
    pallas_call x1, Pallas kernels, weights(): pl.pallas_call(functools.partial(weights_kernel, count), grid=(feats // t...  7.02 us
    pallas_call x1, Pallas kernels, back(): pl.pallas_call(back_kernel, grid_spec=pltpu.PrefetchScalarGridSpec(num_sc...  5.75 us
    unnamed x34, local copies, waits for them, and re-layouts  4.18 us
    pallas_call x1, Pallas kernels, head(): pl.pallas_call(head_kernel, grid=(feats // tile,), in_specs=[whole((rows,...  3.76 us
  transfers between devices with their start and end apart: 26, of which 11 were waited for; matrix products, arithmetic and copies ran while one was open for 0% of the time, Pallas kernels for 11%

profile of v1, /device:TPU:17, one launch (start us, length us, event | category | flops | bytes accessed | tf_op | source)
XLA Modules:
  0.0 174.8 jit_solution(9432290313050018342)
XLA Ops:
  0.6 0.8 collective-permute-start
  1.4 2.1 %collective-permute-start.1 = (bf16[256,768]{1,0:T(8,128)(2,1)}, bf16[256,768]{1,0:T(8,128)(2,1)S(1)}, u32[]{:S(2)}, u32[]{:S(2)}) collective-permute-start(bf16[256,768]{1,0:T(8,128)(2,1)} %bitcast.23), channel_id=1, source_target_pairs={{8,0},{13,1},{2,2},{7,3},{12,4},{9,5},{6,6},{3,7},{0,8},{5,9},{10,... | collective-permute-start | bytes 1179656 | tf_op jit(solution)/shard_map/ppermute | solution.py:308
  3.5 2.6 %collective-permute-start.11 = (bf16[256,1536]{1,0:T(8,128)(2,1)}, bf16[256,1536]{1,0:T(8,128)(2,1)S(1)}, u32[]{:S(2)}, u32[]{:S(2)}) collective-permute-start(bf16[256,1536]{1,0:T(8,128)(2,1)} %bitcast.20), channel_id=1, source_target_pairs={{0,48},{1,49},{2,50},{3,51},{4,52},{5,53},{6,54},{7,55},{8,56},{9,... | collective-permute-start | bytes 2359304 | tf_op jit(solution)/shard_map/ppermute | solution.py:308
  6.0 3.3 %collective-permute-start.4 = (bf16[256,768]{1,0:T(8,128)(2,1)}, bf16[256,768]{1,0:T(8,128)(2,1)S(1)}, u32[]{:S(2)}, u32[]{:S(2)}) collective-permute-start(bf16[256,768]{1,0:T(8,128)(2,1)} %bitcast.24), channel_id=1, source_target_pairs={{9,0},{12,1},{3,2},{6,3},{13,4},{8,5},{7,6},{2,7},{1,8},{4,9},{11,... | collective-permute-start | bytes 1179656 | tf_op jit(solution)/shard_map/ppermute | solution.py:308
  9.3 1.4 copy-done
  10.7 0.7 copy-done.6
  11.4 0.6 pick.1
  12.0 0.0 copy-start.4
  12.0 0.0 copy-start.2
  12.1 8.1 %collective-permute-start.9 = (bf16[256,1536]{1,0:T(8,128)(2,1)S(1)}, bf16[256,1536]{1,0:T(8,128)(2,1)S(1)}, u32[]{:S(2)}, u32[]{:S(2)}) collective-permute-start(bf16[256,1536]{1,0:T(8,128)(2,1)S(1)} %pick.1), channel_id=1, source_target_pairs={{0,192},{1,193},{2,194},{3,195},{4,196},{5,197},{6,198},{7,199},{8... | collective-permute-start | bytes 2359304 | tf_op jit(solution)/shard_map/ppermute | solution.py:308
  20.1 0.7 collective-permute-done.1.a10.refs_5_
  20.9 5.2 %collective-permute-start.2 = (bf16[256,768]{1,0:T(8,128)(2,1)}, bf16[256,768]{1,0:T(8,128)(2,1)S(1)}, u32[]{:S(2)}, u32[]{:S(2)}) collective-permute-start(bf16[256,768]{1,0:T(8,128)(2,1)} %bitcast.26), channel_id=1, source_target_pairs={{0,0},{5,1},{10,2},{15,3},{4,4},{1,5},{14,6},{11,7},{8,8},{13,9},{... | collective-permute-start | bytes 1179656 | tf_op jit(solution)/shard_map/ppermute | solution.py:308
  26.1 0.1 collective-permute-start.6
  26.2 0.5 collective-permute-start.5
  26.7 0.7 collective-permute-start.12
  27.4 4.3 %collective-permute-done.2.a00.refs_4_ = bf16[256,768]{1,0:T(8,128)(2,1)S(1)} collective-permute-done((bf16[256,768]{1,0:T(8,128)(2,1)}, bf16[256,768]{1,0:T(8,128)(2,1)S(1)}, u32[]{:S(2)}, u32[]{:S(2)}) %collective-permute-start.2) | collective-permute-done | bytes 393248 | tf_op jit(solution)/shard_map/ppermute | solution.py:308
  31.7 3.8 %head.1 = (bf16[256,1536]{1,0:T(8,128)(2,1)S(1)}, bf16[256,1536]{1,0:T(8,128)(2,1)S(1)}) custom-call(bf16[256,768]{1,0:T(8,128)(2,1)S(1)} %collective-permute-done.2.a00.refs_4_, bf16[256,768]{1,0:T(8,128)(2,1)S(1)} %collective-permute-done.3.a01, bf16[256,768]{1,0:T(8,128)(2,1)S(1)} %collective-permute-done.1.a10.refs_5_, ...), custom_call_target="tpu_custom_call" | custom-call | flops 2415919104 | bytes 7864320 | tf_op jit(solution)/shard_map/head/pallas_call | solution.py:68
  35.5 0.7 copy-done.11
  36.3 0.7 copy-done.13
  37.0 1.9 %collective-permute-start.7 = (bf16[256,1536]{1,0:T(8,128)(2,1)S(1)}, bf16[256,1536]{1,0:T(8,128)(2,1)S(1)}, u32[]{:S(2)}, u32[]{:S(2)}) collective-permute-start(bf16[256,1536]{1,0:T(8,128)(2,1)S(1)} %get-tuple-element.32), channel_id=1, source_target_pairs={{0,0},{1,4},{2,8},{3,12},{4,5},{5,1},{6,13},{7,9},{8,10},{9,14},{1... | collective-permute-start | bytes 2359304 | tf_op jit(solution)/shard_map/ppermute | solution.py:308
  38.9 5.7 %collective-permute-start.8 = (bf16[256,1536]{1,0:T(8,128)(2,1)S(1)}, bf16[256,1536]{1,0:T(8,128)(2,1)S(1)}, u32[]{:S(2)}, u32[]{:S(2)}) collective-permute-start(bf16[256,1536]{1,0:T(8,128)(2,1)S(1)} %get-tuple-element.33), channel_id=1, source_target_pairs={{0,8},{1,12},{2,0},{3,4},{4,13},{5,9},{6,5},{7,1},{8,2},{9,6},{10,... | collective-permute-start | bytes 2359304 | tf_op jit(solution)/shard_map/ppermute | solution.py:308
  44.7 7.2 %collective-permute-done.9 = bf16[256,1536]{1,0:T(8,128)(2,1)S(1)} collective-permute-done((bf16[256,1536]{1,0:T(8,128)(2,1)S(1)}, bf16[256,1536]{1,0:T(8,128)(2,1)S(1)}, u32[]{:S(2)}, u32[]{:S(2)}) %collective-permute-start.9) | collective-permute-done | bytes 786464 | tf_op jit(solution)/shard_map/ppermute | solution.py:308
  51.8 1.3 collective-permute-start.13
  53.1 17.4 %collective-permute-done.13.gain_ref = f32[1,1536]{1,0:T(1,128)S(1)} collective-permute-done((f32[1,1536]{1,0:T(1,128)S(1)}, f32[1,1536]{1,0:T(1,128)S(1)}, u32[]{:S(2)}, u32[]{:S(2)}) %collective-permute-start.13) | collective-permute-done | bytes 6176 | tf_op jit(solution)/shard_map/ppermute | solution.py:308
  70.6 2.2 %collective-permute-done.7.y0 = bf16[256,1536]{1,0:T(8,128)(2,1)S(1)} collective-permute-done((bf16[256,1536]{1,0:T(8,128)(2,1)S(1)}, bf16[256,1536]{1,0:T(8,128)(2,1)S(1)}, u32[]{:S(2)}, u32[]{:S(2)}) %collective-permute-start.7) | collective-permute-done | bytes 786464 | tf_op jit(solution)/shard_map/ppermute | solution.py:308
  72.8 5.2 %collective-permute-done.8.y1 = bf16[256,1536]{1,0:T(8,128)(2,1)S(1)} collective-permute-done((bf16[256,1536]{1,0:T(8,128)(2,1)S(1)}, bf16[256,1536]{1,0:T(8,128)(2,1)S(1)}, u32[]{:S(2)}, u32[]{:S(2)}) %collective-permute-start.8) | collective-permute-done | bytes 786464 | tf_op jit(solution)/shard_map/ppermute | solution.py:308
  78.0 2.9 %sums.1 = (bf16[256,1536]{1,0:T(8,128)(2,1)S(1)}, bf16[256,1536]{1,0:T(8,128)(2,1)}, f32[16,128]{1,0:T(8,128)S(1)}) custom-call(s32[2]{0:T(128)S(1)} %copy-done.7, bf16[256,1536]{1,0:T(8,128)(2,1)S(1)} %collective-permute-done.7.y0, bf16[256,1536]{1,0:T(8,128)(2,1)S(1)} %collective-permute-done.8.y1, bf16[256,1536]{1,0:T(8,128)(2,1)S(1)} %bitcast.16, ...), custom_call_target="tpu_custom_call" | custom-call | flops 7864320 | bytes 5505024 | tf_op jit(solution)/shard_map/sums/pallas_call | solution.py:126
  81.0 0.3 collective-permute-start.17
  81.3 4.4 %collective-permute-start.16 = (f32[16,128]{1,0:T(8,128)S(1)}, f32[16,128]{1,0:T(8,128)S(1)}, u32[]{:S(2)}, u32[]{:S(2)}) collective-permute-start(f32[16,128]{1,0:T(8,128)S(1)} %get-tuple-element.37.s0), channel_id=1, source_target_pairs={{0,2},{1,3},{2,0},{3,1},{4,6},{5,7},{6,4},{7,5},{8,10},{9,11},{10,... | collective-permute-start | bytes 24584 | tf_op jit(solution)/shard_map/ppermute | solution.py:31
  85.7 0.4 collective-permute-start.15
  86.0 0.9 collective-permute-done.16.s2
  87.0 1.2 norm.1
  88.2 0.6 copy-done.15
  88.7 9.5 %collective-permute-start.20 = (bf16[256,1536]{1,0:T(8,128)(2,1)S(1)}, bf16[256,1536]{1,0:T(8,128)(2,1)}, u32[]{:S(2)}, u32[]{:S(2)}) collective-permute-start(bf16[256,1536]{1,0:T(8,128)(2,1)S(1)} %get-tuple-element.40), channel_id=1, source_target_pairs={{8,0},{12,1},{0,2},{4,3},{13,4},{9,5},{5,6},{1,7},{2,8},{6,9},{10,... | collective-permute-start | bytes 2359304 | tf_op jit(solution)/shard_map/ppermute | solution.py:308
  98.3 2.8 %collective-permute-start.19 = (bf16[256,1536]{1,0:T(8,128)(2,1)S(1)}, bf16[256,1536]{1,0:T(8,128)(2,1)}, u32[]{:S(2)}, u32[]{:S(2)}) collective-permute-start(bf16[256,1536]{1,0:T(8,128)(2,1)S(1)} %get-tuple-element.40), channel_id=1, source_target_pairs={{0,0},{4,1},{8,2},{12,3},{5,4},{1,5},{13,6},{9,7},{10,8},{14,9},{2... | collective-permute-start | bytes 2359304 | tf_op jit(solution)/shard_map/ppermute | solution.py:308
  101.1 17.7 %collective-permute-done.20.refs_1_.g1 = bf16[256,1536]{1,0:T(8,128)(2,1)} collective-permute-done((bf16[256,1536]{1,0:T(8,128)(2,1)S(1)}, bf16[256,1536]{1,0:T(8,128)(2,1)}, u32[]{:S(2)}, u32[]{:S(2)}) %collective-permute-start.20) | collective-permute-done | bytes 786464 | tf_op jit(solution)/shard_map/ppermute | solution.py:308
  118.7 0.7 collective-permute-start.22
  119.5 1.3 collective-permute-done.19.refs_0_.g0
  120.8 1.6 collective-permute-start.21
  122.4 0.1 pad_add_fusion.place
  122.5 2.2 %collective-permute-done.21.refs_2_.g2 = bf16[256,1536]{1,0:T(8,128)(2,1)} collective-permute-done((bf16[256,1536]{1,0:T(8,128)(2,1)}, bf16[256,1536]{1,0:T(8,128)(2,1)}, u32[]{:S(2)}, u32[]{:S(2)}) %collective-permute-start.21) | collective-permute-done | bytes 786464 | tf_op jit(solution)/shard_map/ppermute | solution.py:31
  124.7 5.8 %back.1 = (bf16[256,768]{1,0:T(8,128)(2,1)S(1)}, bf16[256,768]{1,0:T(8,128)(2,1)S(1)}, bf16[256,768]{1,0:T(8,128)(2,1)S(1)}, bf16[256,768]{1,0:T(8,128)(2,1)S(1)}) custom-call(s32[2]{0:T(128)S(1)} %pad_add_fusion.place, bf16[256,1536]{1,0:T(8,128)(2,1)} %collective-permute-done.19.refs_0_.g0, bf16[256,1536]{1,0:T(8,128)(2,1)} %collective-permute-done.20.refs_1_.g1, ...), custom_call_target="tpu_custom_call" | custom-call | flops 2415919104 | bytes 7077888 | tf_op jit(solution)/shard_map/back/pallas_call | solution.py:242
  130.4 1.0 collective-permute-start.23
  131.5 1.7 collective-permute-start.25
  133.2 7.0 %weights.1 = bf16[1536,768]{1,0:T(8,128)(2,1)} custom-call(bf16[256,1536]{1,0:T(8,128)(2,1)} %collective-permute-done.19.refs_0_.g0, bf16[256,1536]{1,0:T(8,128)(2,1)} %collective-permute-done.20.refs_1_.g1, bf16[256,1536]{1,0:T(8,128)(2,1)} %collective-permute-done.21.refs_2_.g2, bf16[256,1536]{1,0:T(8,128)(2,1)} %collective-permute-done.22.refs_3_.g3, ...), custom_call_target="tpu_custom_call" | custom-call | flops 2415919104 | bytes 7077888 | tf_op jit(solution)/shard_map/weights/pallas_call | solution.py:270
  140.3 31.6 %collective-permute-done.18.stat_ref = f32[16,128]{1,0:T(8,128)S(1)} collective-permute-done((f32[16,128]{1,0:T(8,128)S(1)}, f32[16,128]{1,0:T(8,128)S(1)}, u32[]{:S(2)}, u32[]{:S(2)}) %collective-permute-start.18) | collective-permute-done | bytes 8224 | tf_op jit(solution)/shard_map/ppermute | solution.py:308
  171.8 2.0 %finish.1 = (bf16[256,1536]{1,0:T(8,128)(2,1)}, bf16[256,1536]{1,0:T(8,128)(2,1)}) custom-call(s32[2]{0:T(128)S(1)} %copy-done.7, bf16[256,1536]{1,0:T(8,128)(2,1)S(1)} %collective-permute-done.14.delta_ref, bf16[4,128,1536]{2,1,0:T(8,128)(2,1)S(1)} %bitcast.14, f32[16,128]{1,0:T(8,128)S(1)} %collective-permute-done.18.stat_ref, f32[1,1536]{1,0:T(1,128)S(1)} %copy-done.4, ...), custom_call_target="tpu_custom_call" | custom-call | flops 3145728 | bytes 3145728 | tf_op jit(solution)/shard_map/finish/pallas_call | solution.py:208
  173.9 1.0 fusion
  (47 shorter events, 0.1 us)
Async XLA Ops:
  0.6 11.4 %collective-permute-start = (bf16[1536,768]{1,0:T(8,128)(2,1)}, bf16[1536,768]{1,0:T(8,128)(2,1)S(1)}, u32[]{:S(2)}, u32[]{:S(2)}) collective-permute-start(bf16[1536,768]{1,0:T(8,128)(2,1)} %bitcast.17), channel_id=1, source_target_pairs={{0,1},{1,0},{2,3},{3,2},{4,5},{5,4},{6,7},{7,6},{8,9},{9,8},{10,11... | collective-permute-start | bytes 7077896 | tf_op jit(solution)/shard_map/ppermute | solution.py:31
  1.4 19.5 %collective-permute-start.1 = (bf16[256,768]{1,0:T(8,128)(2,1)}, bf16[256,768]{1,0:T(8,128)(2,1)S(1)}, u32[]{:S(2)}, u32[]{:S(2)}) collective-permute-start(bf16[256,768]{1,0:T(8,128)(2,1)} %bitcast.23), channel_id=1, source_target_pairs={{8,0},{13,1},{2,2},{7,3},{12,4},{9,5},{6,6},{3,7},{0,8},{5,9},{10,... | collective-permute-start | bytes 1179656 | tf_op jit(solution)/shard_map/ppermute | solution.py:308
  3.5 23.2 %collective-permute-start.11 = (bf16[256,1536]{1,0:T(8,128)(2,1)}, bf16[256,1536]{1,0:T(8,128)(2,1)S(1)}, u32[]{:S(2)}, u32[]{:S(2)}) collective-permute-start(bf16[256,1536]{1,0:T(8,128)(2,1)} %bitcast.20), channel_id=1, source_target_pairs={{0,48},{1,49},{2,50},{3,51},{4,52},{5,53},{6,54},{7,55},{8,56},{9,... | collective-permute-start | bytes 2359304 | tf_op jit(solution)/shard_map/ppermute | solution.py:308
  6.0 20.0 %collective-permute-start.4 = (bf16[256,768]{1,0:T(8,128)(2,1)}, bf16[256,768]{1,0:T(8,128)(2,1)S(1)}, u32[]{:S(2)}, u32[]{:S(2)}) collective-permute-start(bf16[256,768]{1,0:T(8,128)(2,1)} %bitcast.24), channel_id=1, source_target_pairs={{9,0},{12,1},{3,2},{6,3},{13,4},{8,5},{7,6},{2,7},{1,8},{4,9},{11,... | collective-permute-start | bytes 1179656 | tf_op jit(solution)/shard_map/ppermute | solution.py:308
  9.3 16.9 %collective-permute-start.3 = (bf16[256,768]{1,0:T(8,128)(2,1)}, bf16[256,768]{1,0:T(8,128)(2,1)S(1)}, u32[]{:S(2)}, u32[]{:S(2)}) collective-permute-start(bf16[256,768]{1,0:T(8,128)(2,1)} %bitcast.25), channel_id=1, source_target_pairs={{1,0},{4,1},{11,2},{14,3},{5,4},{0,5},{15,6},{10,7},{9,8},{12,9},{... | collective-permute-start | bytes 1179656 | tf_op jit(solution)/shard_map/ppermute | solution.py:308
  9.3 1.4 copy-start
  10.7 0.7 copy-start.6
  11.4 20.4 %copy-start.8 = (bf16[1,1536,768]{2,1,0:T(8,128)(2,1)S(1)}, bf16[1,1536,768]{2,1,0:T(8,128)(2,1)}, u32[]{:S(2)}) copy-start(bf16[1,1536,768]{2,1,0:T(8,128)(2,1)} %param.10) | copy-start | bytes 7077892
  12.0 39.8 %copy-start.4 = (f32[1,1536]{1,0:T(1,128)S(1)}, f32[1,1536]{1,0:T(1,128)}, u32[]{:S(2)}) copy-start(f32[1,1536]{1,0:T(1,128)} %gain_ref.1) | copy-start | bytes 18436
  12.0 66.0 %copy-start.2 = (bf16[1,4,128,1536]{3,2,1,0:T(8,128)(2,1)S(1)}, bf16[1,4,128,1536]{3,2,1,0:T(8,128)(2,1)}, u32[]{:S(2)}) copy-start(bf16[1,4,128,1536]{3,2,1,0:T(8,128)(2,1)} %param.12) | copy-start | bytes 4718596
  12.0 66.0 %copy-start.3 = (bf16[1,256,1536]{2,1,0:T(8,128)(2,1)S(1)}, bf16[1,256,1536]{2,1,0:T(8,128)(2,1)}, u32[]{:S(2)}) copy-start(bf16[1,256,1536]{2,1,0:T(8,128)(2,1)} %param.11) | copy-start | bytes 2359300
  12.1 66.0 %copy-start.7 = (s32[2]{0:T(128)S(1)}, s32[2]{0:T(128)}, u32[]{:S(2)}) copy-start(s32[2]{0:T(128)} %ids.5) | copy-start | bytes 28
  12.1 39.7 %collective-permute-start.9 = (bf16[256,1536]{1,0:T(8,128)(2,1)S(1)}, bf16[256,1536]{1,0:T(8,128)(2,1)S(1)}, u32[]{:S(2)}, u32[]{:S(2)}) collective-permute-start(bf16[256,1536]{1,0:T(8,128)(2,1)S(1)} %pick.1), channel_id=1, source_target_pairs={{0,192},{1,193},{2,194},{3,195},{4,196},{5,197},{6,198},{7,199},{8... | collective-permute-start | bytes 2359304 | tf_op jit(solution)/shard_map/ppermute | solution.py:308
  20.9 10.8 %collective-permute-start.2 = (bf16[256,768]{1,0:T(8,128)(2,1)}, bf16[256,768]{1,0:T(8,128)(2,1)S(1)}, u32[]{:S(2)}, u32[]{:S(2)}) collective-permute-start(bf16[256,768]{1,0:T(8,128)(2,1)} %bitcast.26), channel_id=1, source_target_pairs={{0,0},{5,1},{10,2},{15,3},{4,4},{1,5},{14,6},{11,7},{8,8},{13,9},{... | collective-permute-start | bytes 1179656 | tf_op jit(solution)/shard_map/ppermute | solution.py:308
  26.1 9.4 %collective-permute-start.6 = (bf16[256,768]{1,0:T(8,128)(2,1)S(1)}, bf16[256,768]{1,0:T(8,128)(2,1)S(1)}, u32[]{:S(2)}, u32[]{:S(2)}) collective-permute-start(bf16[256,768]{1,0:T(8,128)(2,1)S(1)} %collective-permute-done.4.a11), channel_id=1, source_target_pairs={{0,1},{1,0},{2,3},{3,2},{4,5},{5,4},{6,7},{7,6},{8,9},{9,8},{10,11... | collective-permute-start | bytes 1179656 | tf_op jit(solution)/shard_map/ppermute | solution.py:31
  26.2 10.1 %collective-permute-start.5 = (bf16[256,768]{1,0:T(8,128)(2,1)S(1)}, bf16[256,768]{1,0:T(8,128)(2,1)S(1)}, u32[]{:S(2)}, u32[]{:S(2)}) collective-permute-start(bf16[256,768]{1,0:T(8,128)(2,1)S(1)} %collective-permute-done.3.a01), channel_id=1, source_target_pairs={{0,1},{1,0},{2,3},{3,2},{4,5},{5,4},{6,7},{7,6},{8,9},{9,8},{10,11... | collective-permute-start | bytes 1179656 | tf_op jit(solution)/shard_map/ppermute | solution.py:31
  26.7 26.4 %collective-permute-start.12 = (bf16[256,1536]{1,0:T(8,128)(2,1)S(1)}, bf16[256,1536]{1,0:T(8,128)(2,1)S(1)}, u32[]{:S(2)}, u32[]{:S(2)}) collective-permute-start(bf16[256,1536]{1,0:T(8,128)(2,1)S(1)} %collective-permute-done.11), channel_id=1, source_target_pairs={{0,0},{1,1},{2,2},{3,3},{4,4},{5,5},{6,6},{7,7},{8,8},{9,9},{10,10... | collective-permute-start | bytes 2359304 | tf_op jit(solution)/shard_map/ppermute | solution.py:308
  31.7 3.8 %copy-start.9 = (bf16[256,768]{1,0:T(8,128)(2,1)}, bf16[256,768]{1,0:T(8,128)(2,1)S(1)}, u32[]{:S(2)}) copy-start(bf16[256,768]{1,0:T(8,128)(2,1)S(1)} %collective-permute-done.2.a00.refs_4_) | copy-start | bytes 1179652
  35.5 0.7 copy-start.11
  36.3 0.7 copy-start.13
  37.0 35.8 %collective-permute-start.7 = (bf16[256,1536]{1,0:T(8,128)(2,1)S(1)}, bf16[256,1536]{1,0:T(8,128)(2,1)S(1)}, u32[]{:S(2)}, u32[]{:S(2)}) collective-permute-start(bf16[256,1536]{1,0:T(8,128)(2,1)S(1)} %get-tuple-element.32), channel_id=1, source_target_pairs={{0,0},{1,4},{2,8},{3,12},{4,5},{5,1},{6,13},{7,9},{8,10},{9,14},{1... | collective-permute-start | bytes 2359304 | tf_op jit(solution)/shard_map/ppermute | solution.py:308
  38.9 39.1 %collective-permute-start.8 = (bf16[256,1536]{1,0:T(8,128)(2,1)S(1)}, bf16[256,1536]{1,0:T(8,128)(2,1)S(1)}, u32[]{:S(2)}, u32[]{:S(2)}) collective-permute-start(bf16[256,1536]{1,0:T(8,128)(2,1)S(1)} %get-tuple-element.33), channel_id=1, source_target_pairs={{0,8},{1,12},{2,0},{3,4},{4,13},{5,9},{6,5},{7,1},{8,2},{9,6},{10,... | collective-permute-start | bytes 2359304 | tf_op jit(solution)/shard_map/ppermute | solution.py:308
  51.8 26.2 %collective-permute-start.10 = (bf16[256,1536]{1,0:T(8,128)(2,1)S(1)}, bf16[256,1536]{1,0:T(8,128)(2,1)S(1)}, u32[]{:S(2)}, u32[]{:S(2)}) collective-permute-start(bf16[256,1536]{1,0:T(8,128)(2,1)S(1)} %collective-permute-done.9), channel_id=1, source_target_pairs={{0,48},{1,49},{2,50},{3,51},{4,52},{5,53},{6,54},{7,55},{8,56},{9,... | collective-permute-start | bytes 2359304 | tf_op jit(solution)/shard_map/ppermute | solution.py:308
  51.8 18.7 %collective-permute-start.13 = (f32[1,1536]{1,0:T(1,128)S(1)}, f32[1,1536]{1,0:T(1,128)S(1)}, u32[]{:S(2)}, u32[]{:S(2)}) collective-permute-start(f32[1,1536]{1,0:T(1,128)S(1)} %copy-done.4), channel_id=1, source_target_pairs={{0,240},{1,241},{2,242},{3,243},{4,244},{5,245},{6,246},{7,247},{8... | collective-permute-start | bytes 18440 | tf_op jit(solution)/shard_map/ppermute | solution.py:308
  81.0 5.1 %collective-permute-start.17 = (f32[16,128]{1,0:T(8,128)S(1)}, f32[16,128]{1,0:T(8,128)S(1)}, u32[]{:S(2)}, u32[]{:S(2)}) collective-permute-start(f32[16,128]{1,0:T(8,128)S(1)} %get-tuple-element.37.s0), channel_id=1, source_target_pairs={{0,3},{1,2},{2,1},{3,0},{4,7},{5,6},{6,5},{7,4},{8,11},{9,10},{10,... | collective-permute-start | bytes 24584 | tf_op jit(solution)/shard_map/ppermute | solution.py:31
  81.3 5.7 %collective-permute-start.16 = (f32[16,128]{1,0:T(8,128)S(1)}, f32[16,128]{1,0:T(8,128)S(1)}, u32[]{:S(2)}, u32[]{:S(2)}) collective-permute-start(f32[16,128]{1,0:T(8,128)S(1)} %get-tuple-element.37.s0), channel_id=1, source_target_pairs={{0,2},{1,3},{2,0},{3,1},{4,6},{5,7},{6,4},{7,5},{8,10},{9,11},{10,... | collective-permute-start | bytes 24584 | tf_op jit(solution)/shard_map/ppermute | solution.py:31
  85.7 1.3 collective-permute-start.15
  88.1 0.6 copy-start.15
  88.7 30.0 %collective-permute-start.20 = (bf16[256,1536]{1,0:T(8,128)(2,1)S(1)}, bf16[256,1536]{1,0:T(8,128)(2,1)}, u32[]{:S(2)}, u32[]{:S(2)}) collective-permute-start(bf16[256,1536]{1,0:T(8,128)(2,1)S(1)} %get-tuple-element.40), channel_id=1, source_target_pairs={{8,0},{12,1},{0,2},{4,3},{13,4},{9,5},{5,6},{1,7},{2,8},{6,9},{10,... | collective-permute-start | bytes 2359304 | tf_op jit(solution)/shard_map/ppermute | solution.py:308
  98.3 22.5 %collective-permute-start.19 = (bf16[256,1536]{1,0:T(8,128)(2,1)S(1)}, bf16[256,1536]{1,0:T(8,128)(2,1)}, u32[]{:S(2)}, u32[]{:S(2)}) collective-permute-start(bf16[256,1536]{1,0:T(8,128)(2,1)S(1)} %get-tuple-element.40), channel_id=1, source_target_pairs={{0,0},{4,1},{8,2},{12,3},{5,4},{1,5},{13,6},{9,7},{10,8},{14,9},{2... | collective-permute-start | bytes 2359304 | tf_op jit(solution)/shard_map/ppermute | solution.py:308
  118.7 3.8 %collective-permute-start.22 = (bf16[256,1536]{1,0:T(8,128)(2,1)}, bf16[256,1536]{1,0:T(8,128)(2,1)}, u32[]{:S(2)}, u32[]{:S(2)}) collective-permute-start(bf16[256,1536]{1,0:T(8,128)(2,1)} %collective-permute-done.20.refs_1_.g1), channel_id=1, source_target_pairs={{0,1},{1,0},{2,3},{3,2},{4,5},{5,4},{6,7},{7,6},{8,9},{9,8},{10,11... | collective-permute-start | bytes 2359304 | tf_op jit(solution)/shard_map/ppermute | solution.py:31
  120.8 3.9 %collective-permute-start.21 = (bf16[256,1536]{1,0:T(8,128)(2,1)}, bf16[256,1536]{1,0:T(8,128)(2,1)}, u32[]{:S(2)}, u32[]{:S(2)}) collective-permute-start(bf16[256,1536]{1,0:T(8,128)(2,1)} %collective-permute-done.19.refs_0_.g0), channel_id=1, source_target_pairs={{0,1},{1,0},{2,3},{3,2},{4,5},{5,4},{6,7},{7,6},{8,9},{9,8},{10,11... | collective-permute-start | bytes 2359304 | tf_op jit(solution)/shard_map/ppermute | solution.py:31
  122.4 49.4 %collective-permute-start.14 = (bf16[256,1536]{1,0:T(8,128)(2,1)}, bf16[256,1536]{1,0:T(8,128)(2,1)S(1)}, u32[]{:S(2)}, u32[]{:S(2)}) collective-permute-start(bf16[256,1536]{1,0:T(8,128)(2,1)} %get-tuple-element.36), channel_id=1, source_target_pairs={{0,16},{1,17},{2,18},{3,19},{4,20},{5,21},{6,22},{7,23},{8,24},{9,... | collective-permute-start | bytes 2359304 | tf_op jit(solution)/shard_map/ppermute | solution.py:308
  122.5 10.7 %copy-start.16 = (f32[16,128]{1,0:T(8,128)S(1)}, f32[16,128]{1,0:T(8,128)}, u32[]{:S(2)}) copy-start(f32[16,128]{1,0:T(8,128)} %copy-done.15) | copy-start | bytes 24580
  122.5 10.7 %copy-start.10 = (bf16[256,768]{1,0:T(8,128)(2,1)S(1)}, bf16[256,768]{1,0:T(8,128)(2,1)}, u32[]{:S(2)}) copy-start(bf16[256,768]{1,0:T(8,128)(2,1)} %copy-done.9) | copy-start | bytes 1179652
  122.5 10.7 %copy-start.12 = (bf16[256,768]{1,0:T(8,128)(2,1)S(1)}, bf16[256,768]{1,0:T(8,128)(2,1)}, u32[]{:S(2)}) copy-start(bf16[256,768]{1,0:T(8,128)(2,1)} %copy-done.11) | copy-start | bytes 1179652
  122.5 10.7 %copy-start.14 = (bf16[256,768]{1,0:T(8,128)(2,1)S(1)}, bf16[256,768]{1,0:T(8,128)(2,1)}, u32[]{:S(2)}) copy-start(bf16[256,768]{1,0:T(8,128)(2,1)} %copy-done.13) | copy-start | bytes 1179652
  130.4 43.4 %collective-permute-start.23 = (bf16[256,768]{1,0:T(8,128)(2,1)S(1)}, bf16[256,768]{1,0:T(8,128)(2,1)S(1)}, u32[]{:S(2)}, u32[]{:S(2)}) collective-permute-start(bf16[256,768]{1,0:T(8,128)(2,1)S(1)} %get-tuple-element.46), channel_id=1, source_target_pairs={{0,4},{4,0},{8,12},{12,8},{1,5},{5,1},{9,13},{13,9},{2,6},{6,2},{1... | collective-permute-start | bytes 1179656 | tf_op jit(solution)/shard_map/ppermute | solution.py:31
  131.5 42.4 %collective-permute-start.24 = (bf16[256,768]{1,0:T(8,128)(2,1)S(1)}, bf16[256,768]{1,0:T(8,128)(2,1)S(1)}, u32[]{:S(2)}, u32[]{:S(2)}) collective-permute-start(bf16[256,768]{1,0:T(8,128)(2,1)S(1)} %get-tuple-element.47), channel_id=1, source_target_pairs={{0,8},{4,12},{8,0},{12,4},{1,9},{5,13},{9,1},{13,5},{2,10},{6,14},... | collective-permute-start | bytes 1179656 | tf_op jit(solution)/shard_map/ppermute | solution.py:31
  131.5 42.4 %collective-permute-start.25 = (bf16[256,768]{1,0:T(8,128)(2,1)S(1)}, bf16[256,768]{1,0:T(8,128)(2,1)S(1)}, u32[]{:S(2)}, u32[]{:S(2)}) collective-permute-start(bf16[256,768]{1,0:T(8,128)(2,1)S(1)} %get-tuple-element.48), channel_id=1, source_target_pairs={{0,12},{4,8},{8,4},{12,0},{1,13},{5,9},{9,5},{13,1},{2,14},{6,10},... | collective-permute-start | bytes 1179656 | tf_op jit(solution)/shard_map/ppermute | solution.py:31
  133.2 38.6 %copy-start.1 = (bf16[1,4,128,1536]{3,2,1,0:T(8,128)(2,1)S(1)}, bf16[1,4,128,1536]{3,2,1,0:T(8,128)(2,1)}, u32[]{:S(2)}) copy-start(bf16[1,4,128,1536]{3,2,1,0:T(8,128)(2,1)} %param.13) | copy-start | bytes 4718596
  133.2 38.6 %copy-start.5 = (f32[1,1536]{1,0:T(1,128)S(1)}, f32[1,1536]{1,0:T(1,128)}, u32[]{:S(2)}) copy-start(f32[1,1536]{1,0:T(1,128)} %bias_ref.1) | copy-start | bytes 18436
  133.2 38.6 %collective-permute-start.18 = (f32[16,128]{1,0:T(8,128)S(1)}, f32[16,128]{1,0:T(8,128)S(1)}, u32[]{:S(2)}, u32[]{:S(2)}) collective-permute-start(f32[16,128]{1,0:T(8,128)S(1)} %copy-done.16), channel_id=1, source_target_pairs={{0,16},{1,17},{2,18},{3,19},{4,20},{5,21},{6,22},{7,23},{8,24},{9,... | collective-permute-start | bytes 24584 | tf_op jit(solution)/shard_map/ppermute | solution.py:308
